TPU v7x, 32 devices: a whole 2x2x4 slice. The times are simulated.
32 devices in a mesh: fsdp: 16 (over z, x, core), seq: 2 (over y).
Axes of the slice: x: 2, y: 2, z: 4, core: 2. Of those that a mesh axis runs over, the one named last changes fastest.
Arguments:
- latents: bfloat16 [16, 1024, 1152], P('fsdp', 'seq'), may hold values from -6 to 6
- condition: bfloat16 [16, 1152], P('fsdp'), may hold values from -6 to 6
- w_ada: bfloat16 [1152, 6912], P('fsdp'), may hold values from -0.1875 to 0.1875
- b_ada: bfloat16 [6912], P('fsdp'), may hold values from -2 to 2
- w_qkv: bfloat16 [1152, 3456], P('fsdp'), may hold values from -0.1875 to 0.1875
- b_qv: bfloat16 [2304], P('fsdp'), may hold values from -2 to 2
- w_proj: bfloat16 [1152, 1152], P('fsdp'), may hold values from -1.5 to 1.5
- b_proj: bfloat16 [1152], P('fsdp'), may hold values from -2 to 2
- w_fc1: bfloat16 [1152, 4608], P('fsdp'), may hold values from -0.1875 to 0.1875
- b_fc1: bfloat16 [4608], P('fsdp'), may hold values from -2 to 2
- w_fc2: bfloat16 [4608, 1152], P('fsdp'), may hold values from -0.09375 to 0.09375
- b_fc2: bfloat16 [1152], P('fsdp'), may hold values from -2 to 2
- grad_out: bfloat16 [16, 1024, 1152], P('fsdp', 'seq'), may hold values from -6 to 6
Outputs:
- output: bfloat16 [16, 1024, 1152], P('fsdp', 'seq')
- grad_latents: float32 [16, 1024, 1152], P('fsdp', 'seq')
- grad_condition: float32 [16, 1152], P('fsdp')
- grad_w_ada: float32 [1152, 6912], P('fsdp')
- grad_b_ada: float32 [6912], P('fsdp')
- grad_w_qkv: float32 [1152, 3456], P('fsdp')
- grad_b_qv: float32 [2304], P('fsdp')
- grad_w_proj: float32 [1152, 1152], P('fsdp')
- grad_b_proj: float32 [1152], P('fsdp')
- grad_w_fc1: float32 [1152, 4608], P('fsdp')
- grad_b_fc1: float32 [4608], P('fsdp')
- grad_w_fc2: float32 [4608, 1152], P('fsdp')
- grad_b_fc2: float32 [1152], P('fsdp')
All inputs are finite; a program needn't handle non-finite values.
Results may differ from a plain program's by a relative error of at most 0.018.
Values may be sent and summed in bfloat16 or wider, within the bound.
A program may use at most 256 MiB of HBM per device.

v0:
```python
import math

import jax
import jax.numpy as jnp
from jax import lax
from jax.sharding import PartitionSpec as P

HD = 72


def layer_norm(vector):
    centred = vector - jnp.mean(vector, axis=-1, keepdims=True)
    spread = jnp.mean(centred * centred, axis=-1, keepdims=True)
    return centred * lax.rsqrt(spread + 1e-06)


def modulate(vector, shift, scale):
    return layer_norm(vector) * (1.0 + scale[:, None, :]) + shift[:, None, :]


def sigmoid_linear(vector):
    return vector / (1.0 + jnp.exp(-vector))


def gelu_tanh(vector):
    return (
        0.5
        * vector
        * (1.0 + jnp.tanh(0.7978845608028654 * (vector + 0.044715 * vector * vector * vector)))
    )


def per_device(
    latents,
    condition,
    w_ada,
    b_ada,
    w_qkv,
    b_qv,
    w_proj,
    b_proj,
    w_fc1,
    b_fc1,
    w_fc2,
    b_fc2,
    grad_out,
):
    whole = (
        lax.all_gather(w_ada, "fsdp", axis=0, tiled=True),
        lax.all_gather(b_ada, "fsdp", axis=0, tiled=True),
        lax.all_gather(w_qkv, "fsdp", axis=0, tiled=True),
        lax.all_gather(b_qv, "fsdp", axis=0, tiled=True),
        lax.all_gather(w_proj, "fsdp", axis=0, tiled=True),
        lax.all_gather(b_proj, "fsdp", axis=0, tiled=True),
        lax.all_gather(w_fc1, "fsdp", axis=0, tiled=True),
        lax.all_gather(b_fc1, "fsdp", axis=0, tiled=True),
        lax.all_gather(w_fc2, "fsdp", axis=0, tiled=True),
        lax.all_gather(b_fc2, "fsdp", axis=0, tiled=True),
    )
    (
        full_ada,
        bias_ada,
        full_qkv,
        bias_qv,
        full_proj,
        bias_proj,
        full_fc1,
        bias_fc1,
        full_fc2,
        bias_fc2,
    ) = whole
    model_width = full_qkv.shape[0]
    lat_group = latents.shape[0]
    tok_rows = latents.shape[1]
    cond_float = condition.astype(jnp.float32)
    cond_act = sigmoid_linear(cond_float).astype(jnp.bfloat16)
    modulation = jnp.dot(cond_act, full_ada, preferred_element_type=jnp.float32) + bias_ada.astype(
        jnp.float32
    )
    shift_a, scale_a, gate_a, shift_m, scale_m, gate_m = jnp.split(modulation, 6, axis=1)
    tokens = latents.astype(jnp.float32)
    normed = modulate(tokens, shift_a, scale_a).astype(jnp.bfloat16)
    bias_all = jnp.concatenate(
        [
            bias_qv[:model_width].astype(jnp.float32),
            jnp.zeros((model_width,), jnp.float32),
            bias_qv[model_width:].astype(jnp.float32),
        ]
    )
    joined = (
        jnp.einsum("btd,de->bte", normed, full_qkv, preferred_element_type=jnp.float32) + bias_all
    )
    joined = joined.astype(jnp.bfloat16).reshape(lat_group, tok_rows, 3, model_width)
    head_parts = lax.all_to_all(joined, "seq", split_axis=3, concat_axis=1, tiled=True)
    length = head_parts.shape[1]
    local_heads = head_parts.shape[3] // HD
    query = head_parts[:, :, 0].reshape(lat_group, length, local_heads, HD)
    key_rows = head_parts[:, :, 1].reshape(lat_group, length, local_heads, HD)
    values = head_parts[:, :, 2].reshape(lat_group, length, local_heads, HD)
    factor = 1.0 / math.sqrt(HD)
    block_rows = min(512, length)
    block_count = length // block_rows

    def attend_block(index):
        query_block = lax.dynamic_slice_in_dim(query, index * block_rows, block_rows, 1)
        scores = (
            jnp.einsum("bqhd,bkhd->bhqk", query_block, key_rows, preferred_element_type=jnp.float32)
            * factor
        )
        row_max = jnp.max(scores, axis=-1, keepdims=True)
        exponent = jnp.exp(scores - row_max)
        totals = jnp.sum(exponent, axis=-1, keepdims=True)
        probs_low = (exponent / totals).astype(jnp.bfloat16)
        mixture = jnp.einsum(
            "bhqk,bkhd->bqhd", probs_low, values, preferred_element_type=jnp.float32
        )
        return (mixture.astype(jnp.bfloat16), (row_max + jnp.log(totals))[..., 0])

    mixtures, lse_blocks = lax.map(attend_block, jnp.arange(block_count))
    mixed = jnp.moveaxis(mixtures, 0, 1).reshape(lat_group, length, local_heads * HD)
    attended = lax.all_to_all(mixed, "seq", split_axis=1, concat_axis=2, tiled=True)
    branch_a = jnp.einsum(
        "btd,de->bte", attended, full_proj, preferred_element_type=jnp.float32
    ) + bias_proj.astype(jnp.float32)
    middle = tokens + gate_a[:, None, :] * branch_a
    normed_m = modulate(middle, shift_m, scale_m).astype(jnp.bfloat16)
    hidden = jnp.einsum(
        "btd,df->btf", normed_m, full_fc1, preferred_element_type=jnp.float32
    ) + bias_fc1.astype(jnp.float32)
    active = gelu_tanh(hidden).astype(jnp.bfloat16)
    branch_m = jnp.einsum(
        "btf,fd->btd", active, full_fc2, preferred_element_type=jnp.float32
    ) + bias_fc2.astype(jnp.float32)
    output = (middle + gate_m[:, None, :] * branch_m).astype(jnp.bfloat16)
    cotangent = grad_out.astype(jnp.float32)
    d_gate_m = jnp.sum(cotangent * branch_m, axis=1)
    d_branch_m = (gate_m[:, None, :] * cotangent).astype(jnp.bfloat16)
    grad_fc2 = jnp.einsum("btf,btd->fd", active, d_branch_m, preferred_element_type=jnp.float32)
    grad_bias_fc2 = jnp.sum(d_branch_m, axis=(0, 1), dtype=jnp.float32)
    d_active = jnp.einsum("btd,fd->btf", d_branch_m, full_fc2, preferred_element_type=jnp.float32)
    gelu_unused, gelu_pull = jax.vjp(gelu_tanh, hidden)
    d_hidden = gelu_pull(d_active)[0].astype(jnp.bfloat16)
    grad_fc1 = jnp.einsum("btd,btf->df", normed_m, d_hidden, preferred_element_type=jnp.float32)
    grad_bias_fc1 = jnp.sum(d_hidden, axis=(0, 1), dtype=jnp.float32)
    d_normed_m = jnp.einsum("btf,df->btd", d_hidden, full_fc1, preferred_element_type=jnp.float32)
    norm_unused, pull_second = jax.vjp(modulate, middle, shift_m, scale_m)
    d_middle_norm, d_shift_m, d_scale_m = pull_second(d_normed_m)
    d_middle = cotangent + d_middle_norm
    d_gate_a = jnp.sum(d_middle * branch_a, axis=1)
    d_branch_a = (gate_a[:, None, :] * d_middle).astype(jnp.bfloat16)
    grad_proj = jnp.einsum("btd,bte->de", attended, d_branch_a, preferred_element_type=jnp.float32)
    grad_bias_proj = jnp.sum(d_branch_a, axis=(0, 1), dtype=jnp.float32)
    d_attended = jnp.einsum(
        "bte,de->btd", d_branch_a, full_proj, preferred_element_type=jnp.float32
    ).astype(jnp.bfloat16)
    grad_parts = lax.all_to_all(d_attended, "seq", split_axis=2, concat_axis=1, tiled=True)
    d_mixed = grad_parts.reshape(lat_group, length, local_heads, HD)

    def revisit_block(carry, inputs):
        d_key_acc, d_value_acc = carry
        index, lse_block = inputs
        query_block = lax.dynamic_slice_in_dim(query, index * block_rows, block_rows, 1)
        grad_block = lax.dynamic_slice_in_dim(d_mixed, index * block_rows, block_rows, 1)
        scores = (
            jnp.einsum("bqhd,bkhd->bhqk", query_block, key_rows, preferred_element_type=jnp.float32)
            * factor
        )
        probs = jnp.exp(scores - lse_block[..., None])
        d_probs = jnp.einsum(
            "bqhd,bkhd->bhqk", grad_block, values, preferred_element_type=jnp.float32
        )
        centre = jnp.sum(probs * d_probs, axis=-1, keepdims=True)
        d_scores = (probs * (d_probs - centre)).astype(jnp.bfloat16)
        d_query_block = (
            jnp.einsum("bhqk,bkhd->bqhd", d_scores, key_rows, preferred_element_type=jnp.float32)
            * factor
        )
        d_key_acc = (
            d_key_acc
            + jnp.einsum(
                "bhqk,bqhd->bkhd", d_scores, query_block, preferred_element_type=jnp.float32
            )
            * factor
        )
        d_value_acc = d_value_acc + jnp.einsum(
            "bhqk,bqhd->bkhd",
            probs.astype(jnp.bfloat16),
            grad_block,
            preferred_element_type=jnp.float32,
        )
        return ((d_key_acc, d_value_acc), d_query_block)

    zero_acc = jnp.zeros((lat_group, length, local_heads, HD), jnp.float32)
    (d_keys, d_values), d_query_blocks = lax.scan(
        revisit_block, (zero_acc, zero_acc), (jnp.arange(block_count), lse_blocks)
    )
    d_query = jnp.moveaxis(d_query_blocks, 0, 1).reshape(lat_group, length, local_heads, HD)
    stacked = jnp.stack(
        [d_query.astype(jnp.bfloat16), d_keys.astype(jnp.bfloat16), d_values.astype(jnp.bfloat16)],
        axis=2,
    )
    stacked = stacked.reshape(lat_group, length, 3, local_heads * HD)
    d_joined = lax.all_to_all(stacked, "seq", split_axis=1, concat_axis=3, tiled=True).reshape(
        lat_group, tok_rows, 3 * model_width
    )
    grad_qkv = jnp.einsum("btd,bte->de", normed, d_joined, preferred_element_type=jnp.float32)
    column_sums = jnp.sum(d_joined, axis=(0, 1), dtype=jnp.float32)
    grad_bias_qv = jnp.concatenate([column_sums[:model_width], column_sums[2 * model_width :]])
    d_normed_a = jnp.einsum("bte,de->btd", d_joined, full_qkv, preferred_element_type=jnp.float32)
    first_unused, pull_first = jax.vjp(modulate, tokens, shift_a, scale_a)
    d_tokens_norm, d_shift_a, d_scale_a = pull_first(d_normed_a)
    grad_latents = d_middle + d_tokens_norm
    d_mod_part = jnp.concatenate(
        [d_shift_a, d_scale_a, d_gate_a, d_shift_m, d_scale_m, d_gate_m], axis=1
    )
    summed = (
        lax.psum(d_mod_part.astype(jnp.bfloat16), "seq").astype(jnp.float32),
        lax.psum(grad_bias_qv.astype(jnp.bfloat16), "seq").astype(jnp.float32),
        lax.psum(grad_bias_proj.astype(jnp.bfloat16), "seq").astype(jnp.float32),
        lax.psum(grad_bias_fc1.astype(jnp.bfloat16), "seq").astype(jnp.float32),
        lax.psum(grad_bias_fc2.astype(jnp.bfloat16), "seq").astype(jnp.float32),
    )
    d_modulation = summed[0].astype(jnp.bfloat16)
    silu_unused, silu_pull = jax.vjp(sigmoid_linear, cond_float)
    grad_condition = silu_pull(
        jnp.einsum("be,de->bd", d_modulation, full_ada, preferred_element_type=jnp.float32)
    )[0]
    grad_bias_ada = jnp.sum(d_modulation, axis=0, dtype=jnp.float32)
    ada_term = jnp.einsum("bd,be->de", cond_act, d_modulation, preferred_element_type=jnp.float32)
    ada_owned = lax.psum_scatter(
        ada_term.astype(jnp.bfloat16), "fsdp", scatter_dimension=0, tiled=True
    ).astype(jnp.float32)
    owned = (
        lax.psum_scatter(
            grad_qkv.astype(jnp.bfloat16), "fsdp", scatter_dimension=0, tiled=True
        ).astype(jnp.float32),
        lax.psum_scatter(
            grad_proj.astype(jnp.bfloat16), "fsdp", scatter_dimension=0, tiled=True
        ).astype(jnp.float32),
        lax.psum_scatter(
            grad_fc1.astype(jnp.bfloat16), "fsdp", scatter_dimension=0, tiled=True
        ).astype(jnp.float32),
        lax.psum_scatter(
            grad_fc2.astype(jnp.bfloat16), "fsdp", scatter_dimension=0, tiled=True
        ).astype(jnp.float32),
    )
    owned = (
        lax.psum_scatter(
            owned[0].astype(jnp.bfloat16), "seq", scatter_dimension=1, tiled=True
        ).astype(jnp.float32),
        lax.psum_scatter(
            owned[1].astype(jnp.bfloat16), "seq", scatter_dimension=1, tiled=True
        ).astype(jnp.float32),
        lax.psum_scatter(
            owned[2].astype(jnp.bfloat16), "seq", scatter_dimension=1, tiled=True
        ).astype(jnp.float32),
        lax.psum_scatter(
            owned[3].astype(jnp.bfloat16), "seq", scatter_dimension=1, tiled=True
        ).astype(jnp.float32),
    )
    owned = (
        lax.all_gather(owned[0].astype(jnp.bfloat16), "seq", axis=1, tiled=True).astype(
            jnp.float32
        ),
        lax.all_gather(owned[1].astype(jnp.bfloat16), "seq", axis=1, tiled=True).astype(
            jnp.float32
        ),
        lax.all_gather(owned[2].astype(jnp.bfloat16), "seq", axis=1, tiled=True).astype(
            jnp.float32
        ),
        lax.all_gather(owned[3].astype(jnp.bfloat16), "seq", axis=1, tiled=True).astype(
            jnp.float32
        ),
    )
    bias_owned = (
        lax.psum_scatter(
            grad_bias_ada.astype(jnp.bfloat16), "fsdp", scatter_dimension=0, tiled=True
        ).astype(jnp.float32),
        lax.psum_scatter(
            summed[1].astype(jnp.bfloat16), "fsdp", scatter_dimension=0, tiled=True
        ).astype(jnp.float32),
        lax.psum_scatter(
            summed[2].astype(jnp.bfloat16), "fsdp", scatter_dimension=0, tiled=True
        ).astype(jnp.float32),
        lax.psum_scatter(
            summed[3].astype(jnp.bfloat16), "fsdp", scatter_dimension=0, tiled=True
        ).astype(jnp.float32),
        lax.psum_scatter(
            summed[4].astype(jnp.bfloat16), "fsdp", scatter_dimension=0, tiled=True
        ).astype(jnp.float32),
    )
    return (
        output,
        grad_latents,
        grad_condition,
        ada_owned,
        bias_owned[0],
        owned[0],
        bias_owned[1],
        owned[1],
        bias_owned[2],
        owned[2],
        bias_owned[3],
        owned[3],
        bias_owned[4],
    )


def solution(mesh):
    return jax.shard_map(
        per_device,
        mesh=mesh,
        in_specs=(
            P("fsdp", "seq", None),
            P("fsdp", None),
            P("fsdp", None),
            P("fsdp"),
            P("fsdp", None),
            P("fsdp"),
            P("fsdp", None),
            P("fsdp"),
            P("fsdp", None),
            P("fsdp"),
            P("fsdp", None),
            P("fsdp"),
            P("fsdp", "seq", None),
        ),
        out_specs=(
            P("fsdp", "seq", None),
            P("fsdp", "seq", None),
            P("fsdp", None),
            P("fsdp", None),
            P("fsdp"),
            P("fsdp", None),
            P("fsdp"),
            P("fsdp", None),
            P("fsdp"),
            P("fsdp", None),
            P("fsdp"),
            P("fsdp", None),
            P("fsdp"),
        ),
        check_vma=False,
    )
```

profile of v0, /device:TPU:0, one launch (start us, length us, event | category | flops | bytes accessed | tf_op | source)
XLA Modules:
  0.0 1313.7 jit_solution(16120617942173470715)
XLA Ops:
  15.1 65.9 %all-reduce.13 = (bf16[2304]{0:T(1024)(128)(2,1)S(1)}, bf16[6912]{0:T(1024)(128)(2,1)S(1)}, bf16[1152]{0:T(1024)(128)(2,1)}, bf16[1152]{0:T(1024)(128)(2,1)}, bf16[4608]{0:T(1024)(128)(2,1)}) all-reduce(bf16[2304]{0:T(1024)(128)(2,1)S(1)} %dynamic-update-slice.1, ...), channel_id=1, replica_groups=mesh['fsdp'=16,'seq'=2] {'fsdp'}, use_global_device_ids=true, to_apply=%add.1 | all-reduce | flops 16128 | bytes 64512
  81.8 53.2 %all-gather.9.cloned.1.call-done = bf16[1152,6912]{1,0:T(8,128)(2,1)} async-done(((bf16[72,6912]{1,0:T(8,128)(2,1)}), bf16[1152,6912]{1,0:T(8,128)(2,1)}) %all-gather.9.cloned.1.call-update) | async-done | bytes 15925264 | tf_op jit(solution)/shard_map/all_gather | solution.py:49
  143.5 64.3 %all-gather.11.cloned.1.call-done = bf16[1152,3456]{1,0:T(8,128)(2,1)} async-done(((bf16[72,3456]{1,0:T(8,128)(2,1)}), bf16[1152,3456]{1,0:T(8,128)(2,1)}) %all-gather.11.cloned.1.call-update) | async-done | bytes 7962640 | tf_op jit(solution)/shard_map/all_gather | solution.py:51
  222.1 15.9 %copy.96 = bf16[1,512,3,1152]{1,2,0,3:T(4,128)(2,1)} copy(bf16[1,512,3,1152]{1,3,2,0:T(8,128)(2,1)S(1)} %bitcast.256) | data formatting | bytes 7077888 | tf_op jit(solution)/shard_map/reshape | solution.py:93
  244.1 53.6 %all-to-all-done = bf16[1,512,3,1152]{1,2,0,3:T(4,128)(2,1)} async-done(((bf16[1,512,3,1152]{1,2,0,3:T(4,128)(2,1)}), bf16[1,512,3,1152]{1,2,0,3:T(4,128)(2,1)}, u32[]{:S(2)}, u32[]{:S(2)}) %all-to-all-start) | async-done | bytes 3538976 | tf_op jit(solution)/shard_map/all_to_all | solution.py:94
  303.5 27.5 %while.27 = (s32[]{:T(128)}, bf16[2,1,512,8,72]{2,4,3,1,0:T(8,128)(2,1)S(1)}, f32[2,1,8,512]{3,2,1,0:T(8,128)S(1)}, s32[2]{0:T(128)S(1)}, bf16[1,1024,8,72]{1,3,...) while((s32[]{:T(128)}, ...), condition=%wide.region_5.6_spmd, body=%wide.region_2.5_spmd.sunk | while | flops 1245999104 | bytes 54001840 | solution.py:119
  362.8 14.3 %all-to-all-done.1 = bf16[2,2,147456]{2,1,0:T(2,128)(2,1)} async-done(((bf16[2,2,147456]{2,1,0:T(2,128)(2,1)}), bf16[2,2,147456]{2,1,0:T(2,128)(2,1)}, u32[]{:S(2)}, u32[]{:S(2)}) %all-to-all-start.1) | async-done | bytes 1179680 | tf_op jit(solution)/shard_map/all_to_all | solution.py:121
  392.9 13.0 fusion.86
  405.9 24.3 %all-gather.17.cloned.1.call-done = bf16[4608,1152]{1,0:T(8,128)(2,1)} async-done(((bf16[288,1152]{1,0:T(8,128)(2,1)}), bf16[4608,1152]{1,0:T(8,128)(2,1)}) %all-gather.17.cloned.1.call-update) | async-done | bytes 10616848 | tf_op jit(solution)/shard_map/all_gather | solution.py:57
  430.3 17.8 %fusion.94 = (bf16[4608]{0:T(1024)(128)(2,1)}, bf16[512,4608]{1,0:T(8,128)(2,1)S(1)}) fusion(bf16[4608,1152]{1,0:T(8,128)(2,1)} %all-gather.17.cloned.1.call-done, bf16[1,512,1152]{2,1,0:T(8,128)(2,1)S(1)} %copy-done.15, f32[1152]{0:T(1024)S(1)} %copy-done.23, f32[512,4608]{1,0:T(8,128)} %fusion.86, f32[4608]{0:T(1024)} %convert_element_type.215), kind=kOutput, calls=%fused_computation.158 | convolution fusion | flops 5498924544 | bytes 25984512 | tf_op jit(solution)/shard_map/btd,fd->btf/dot_general | solution.py:140
  448.1 12.8 fusion.59
  487.5 12.3 all-to-all-done.2
  504.5 96.2 %while.28 = (s32[]{:T(128)}, f32[1,1024,8,72]{1,3,2,0:T(8,128)}, f32[1,1024,8,72]{1,3,2,0:T(8,128)}, bf16[2,1,512,8,72]{2,4,3,1,0:T(8,128)(2,1)}, s32[2]{0:T(128...) while((s32[]{:T(128)}, f32[1,1024,8,72]{1,3,2,0:T(8,128)}, ...), condition=%wide.region_12.13_spmd.clone, body=%wide.region_10.12_spmd.clone.sunk | while | flops 3073470464 | bytes 278774720 | solution.py:194
  613.7 66.9 %all_to_all.63 = bf16[1,1024,3,576]{3,2,0,1:T(4,128)(2,1)} all-to-all(bf16[1,1024,3,576]{3,2,0,1:T(4,128)(2,1)} %copy.106), channel_id=1, replica_groups=mesh['fsdp'=16,'seq'=2] {'seq'}, dimensions={1} | all-to-all | bytes 7077888 | tf_op jit(solution)/shard_map/all_to_all | solution.py:203
  680.6 14.9 %copy.116 = bf16[1,2,512,3,576]{2,1,4,3,0:T(2,128)(2,1)S(1)} copy(bf16[1,2,512,3,576]{4,3,2,1,0:T(4,128)(2,1)} %bitcast.254) | data formatting | bytes 7077888 | tf_op jit(solution)/shard_map/all_to_all | solution.py:203
  706.1 11.1 convolution_convert_fusion.1
  718.0 14.3 %convolution_convert_fusion = bf16[4608,1152]{1,0:T(8,128)(2,1)} fusion(bf16[1,512,1152]{2,1,0:T(8,128)(2,1)} %param.29, f32[1152]{0:T(1024)S(1)} %copy-done.24, f32[512,4608]{1,0:T(8,128)} %fusion.86, f32[4608]{0:T(1024)} %convert_element_type.215), kind=kOutput, calls=%fused_computation.48 | convolution fusion | flops 5466488832 | bytes 21256704 | tf_op jit(solution)/shard_map/btf,btd->fd/dot_general | solution.py:138
  754.6 49.3 %reduce-scatter.34.cloned.1.call-done = bf16[72,3456]{1,0:T(8,128)(2,1)} async-done(((bf16[1152,3456]{1,0:T(8,128)(2,1)}), bf16[72,3456]{1,0:T(8,128)(2,1)}) %reduce-scatter.34.cloned.1.call-update) | async-done | bytes 497680
  806.2 18.2 %fusion.58 = (bf16[1152]{0:T(1024)(128)(2,1)}, bf16[1152]{0:T(1024)(128)(2,1)}, f32[1,512,1152]{2,1,0:T(8,128)}, bf16[1,512,1152]{2,1,0:T(8,128)(2,1)}) fusion(bf16[1,512,1152]{2,1,0:T(8,128)(2,1)} %param.29, f32[512,1152]{1,0:T(8,128)} %get-tuple-element.225, f32[1,512,1152]{2,1,0:T(8,128)} %copy-done.9, f32[512]{0:T(512)} %copy-done.44, ...), kind=kOutput, calls=%fused_computation.89 | convolution fusion | flops 5471205376 | bytes 35436544 | tf_op jit(solution)/shard_map/btf,fd->btd/dot_general | solution.py:131
  826.6 101.5 %reduce-scatter.22.cloned.1.call-done = bf16[72,4608]{1,0:T(8,128)(2,1)} async-done(((bf16[1152,4608]{1,0:T(8,128)(2,1)}), bf16[72,4608]{1,0:T(8,128)(2,1)}) %reduce-scatter.22.cloned.1.call-update) | async-done | bytes 663568 | tf_op jit(solution)/shard_map/reduce_scatter | solution.py:240
  943.9 108.2 %reduce-scatter.26.cloned.1.call-done = bf16[288,1152]{1,0:T(8,128)(2,1)} async-done(((bf16[4608,1152]{1,0:T(8,128)(2,1)}), bf16[288,1152]{1,0:T(8,128)(2,1)}) %reduce-scatter.26.cloned.1.call-update) | async-done | bytes 663568 | tf_op jit(solution)/shard_map/reduce_scatter | solution.py:243
  1068.0 60.9 %all-reduce.12 = (bf16[6912]{0:T(1024)(128)(2,1)S(1)}, bf16[2304]{0:T(1024)(128)(2,1)S(1)}, bf16[1152]{0:T(1024)(128)(2,1)S(1)}, bf16[4608]{0:T(1024)(128)(2,1)S(1)}, bf16[1152]{0:T(1024)(128)(2,1)S(1)}) all-reduce(bf16[6912]{0:T(1024)(128)(2,1)S(1)} %psum.35, ...), channel_id=3, replica_groups=mesh['fsdp'=16,'seq'=2] {'fsdp'}, use_global_device_ids=true, to_apply=%region_23.24.clone | all-reduce | flops 16128 | bytes 64512
  1137.0 12.6 negate_add_fusion
  1194.7 109.7 %reduce-scatter.20.cloned.1.call-done = bf16[72,6912]{1,0:T(8,128)(2,1)} async-done(((bf16[1152,6912]{1,0:T(8,128)(2,1)}), bf16[72,6912]{1,0:T(8,128)(2,1)}) %reduce-scatter.20.cloned.1.call-update) | async-done | bytes 995344 | tf_op jit(solution)/shard_map/reduce_scatter | solution.py:230
  (329 shorter events, 375.5 us)
Async XLA Ops:
  7.2 73.9 %copy-start.6 = (bf16[1,512,1152]{2,1,0:T(8,128)(2,1)S(1)}, bf16[1,512,1152]{2,1,0:T(8,128)(2,1)}, u32[]{:S(2)}) copy-start(bf16[1,512,1152]{2,1,0:T(8,128)(2,1)} %param.17) | copy-start | bytes 3538948
  7.3 127.8 %all-gather.9.cloned.1.call-start = ((), (), s32[]{:S(2)}) async-start(), calls=%async_computation.13 | async-start | bytes 16920576 | tf_op jit(solution)/shard_map/all_gather | solution.py:49
  8.0 127.0 %copy-start.21 = (bf16[1,1152]{1,0:T(2,128)(2,1)S(1)}, bf16[1,1152]{1,0:T(2,128)(2,1)}, u32[]{:S(2)}) copy-start(bf16[1,1152]{1,0:T(2,128)(2,1)} %param.18) | copy-start | bytes 6916
  8.0 199.8 %all-gather.11.cloned.1.call-start = ((), (), s32[]{:S(2)}) async-start(), calls=%async_computation.14 | async-start | bytes 8460288 | tf_op jit(solution)/shard_map/all_gather | solution.py:51
  8.8 377.3 %all-gather.13.cloned.1.call-start = ((), (), s32[]{:S(2)}) async-start(), calls=%async_computation.15 | async-start | bytes 2820096 | tf_op jit(solution)/shard_map/all_gather | solution.py:53
  9.5 383.4 %all-gather.15.cloned.1.call-start = ((), (), s32[]{:S(2)}) async-start(), calls=%async_computation.16 | async-start | bytes 11280384 | tf_op jit(solution)/shard_map/all_gather | solution.py:55
  10.1 420.2 %all-gather.17.cloned.1.call-start = ((), (), s32[]{:S(2)}) async-start(), calls=%async_computation.17 | async-start | bytes 11280384 | tf_op jit(solution)/shard_map/all_gather | solution.py:57
  81.3 126.5 %copy-start.30 = (f32[512]{0:T(512)}, f32[512]{0:T(512)S(1)}, u32[]{:S(2)}) copy-start(f32[512]{0:T(512)S(1)} %broadcast_multiply_fusion.1) | copy-start | bytes 6148
  81.8 126.0 %copy-start.39 = (f32[512]{0:T(512)}, f32[512]{0:T(512)S(1)}, u32[]{:S(2)}) copy-start(f32[512]{0:T(512)S(1)} %fusion.80) | copy-start | bytes 6148
  238.1 59.7 %all-to-all-start = ((bf16[1,512,3,1152]{1,2,0,3:T(4,128)(2,1)}), bf16[1,512,3,1152]{1,2,0,3:T(4,128)(2,1)}, u32[]{:S(2)}, u32[]{:S(2)}) async-start(bf16[1,512,3,1152]{1,2,0,3:T(4,128)(2,1)} %copy.96), calls=%async_computation | async-start | bytes 9437184 | tf_op jit(solution)/shard_map/all_to_all | solution.py:94
  357.7 19.4 %all-to-all-start.1 = ((bf16[2,2,147456]{2,1,0:T(2,128)(2,1)}), bf16[2,2,147456]{2,1,0:T(2,128)(2,1)}, u32[]{:S(2)}, u32[]{:S(2)}) async-start(bf16[2,2,147456]{2,1,0:T(2,128)(2,1)} %reshape.624), calls=%async_computation.1 | async-start | bytes 2359296 | tf_op jit(solution)/shard_map/all_to_all | solution.py:121
  480.5 19.3 %all-to-all-start.2 = ((bf16[2,2,147456]{2,1,0:T(2,128)(2,1)}), bf16[2,2,147456]{2,1,0:T(2,128)(2,1)S(1)}, u32[]{:S(2)}, u32[]{:S(2)}) async-start(bf16[2,2,147456]{2,1,0:T(2,128)(2,1)} %reshape.626), calls=%async_computation.2 | async-start | bytes 2359296 | tf_op jit(solution)/shard_map/all_to_all | solution.py:156
  484.1 264.4 %reduce-scatter.36.cloned.1.call-start = ((), (), s32[]{:S(2)}) async-start(), calls=%async_computation.26 | async-start | bytes 2820096
  487.5 316.4 %reduce-scatter.34.cloned.1.call-start = ((), (), s32[]{:S(2)}) async-start(), calls=%async_computation.25 | async-start | bytes 8460288
  705.5 222.6 %reduce-scatter.22.cloned.1.call-start = ((), (), s32[]{:S(2)}) async-start(), calls=%async_computation.19 | async-start | bytes 11280384 | tf_op jit(solution)/shard_map/reduce_scatter | solution.py:240
  717.3 334.8 %reduce-scatter.26.cloned.1.call-start = ((), (), s32[]{:S(2)}) async-start(), calls=%async_computation.21 | async-start | bytes 11280384 | tf_op jit(solution)/shard_map/reduce_scatter | solution.py:243
  732.3 417.3 %reduce-scatter.30.cloned.1.call-start = ((), (), s32[]{:S(2)}) async-start(), calls=%async_computation.23 | async-start | bytes 442368
  750.4 407.5 %reduce-scatter.28.cloned.1.call-start = ((), (), s32[]{:S(2)}) async-start(), calls=%async_computation.22 | async-start | bytes 1327104
  806.2 364.6 %reduce-scatter.24.cloned.1.call-start = ((), (), s32[]{:S(2)}) async-start(), calls=%async_computation.20 | async-start | bytes 995328 | tf_op jit(solution)/shard_map/reduce_scatter | solution.py:254
  824.5 104.3 %copy-start.42 = (bf16[1152]{0:T(1024)(128)(2,1)S(1)}, bf16[1152]{0:T(1024)(128)(2,1)}, u32[]{:S(2)}) copy-start(bf16[1152]{0:T(1024)(128)(2,1)} %get-tuple-element.145) | copy-start | bytes 6916
  824.5 106.1 %copy-start.41 = (bf16[1152]{0:T(1024)(128)(2,1)S(1)}, bf16[1152]{0:T(1024)(128)(2,1)}, u32[]{:S(2)}) copy-start(bf16[1152]{0:T(1024)(128)(2,1)} %reduce_sum.212) | copy-start | bytes 6916
  824.5 106.7 %copy-start.50 = (bf16[1152]{0:T(1024)(128)(2,1)S(1)}, bf16[1152]{0:T(1024)(128)(2,1)}, u32[]{:S(2)}) copy-start(bf16[1152]{0:T(1024)(128)(2,1)} %get-tuple-element.143) | copy-start | bytes 6916
  928.1 254.6 %reduce-scatter.32.cloned.1.call-start = ((), (), s32[]{:S(2)}) async-start(), calls=%async_computation.24 | async-start | bytes 1327104
  1054.5 249.9 %reduce-scatter.20.cloned.1.call-start = ((), (), s32[]{:S(2)}) async-start(), calls=%async_computation.18 | async-start | bytes 16920576 | tf_op jit(solution)/shard_map/reduce_scatter | solution.py:230
  (62 other events, 685.7 us)
Sparse Core Ops, SparseCore 0:
  10.3 124.7 all-gather.8
  137.2 70.5 all-gather.10
  210.0 41.6 all-gather.12
  253.8 87.3 all-gather.14
  343.3 86.8 all-gather.16
  488.6 62.6 reduce-scatter.35
  705.6 98.2 reduce-scatter.33
  808.0 120.0 reduce-scatter.21
  932.1 119.9 reduce-scatter.25
  1054.8 11.7 reduce-scatter.29
  1069.5 18.5 reduce-scatter.27
  1090.2 16.0 reduce-scatter.23
  1109.2 18.4 reduce-scatter.31
  1132.3 171.9 reduce-scatter.19
where the time goes:
time: 1320 us; the launch traced here: 1310 us
  waiting for transfers between devices  594 us (45%)
  blocking collectives  242 us (18%)
  matrix products  233 us (18%)
  local copies, waits for them, and re-layouts  125 us (9%)
  other arithmetic  81.7 us (6%)
  between operations  20 us (2%)
  starting transfers between devices  14.7 us (1%)
    unnamed x2, blocking collectives  127 us
    reduce_scatter x1, waiting for transfers between devices, per_device(): lax.psum_scatter(ada_term.astype(jnp.bfloat16), 'fsdp', scatter_dimension...  110 us
    reduce_scatter x1, waiting for transfers between devices, per_device(): lax.psum_scatter(grad_fc2.astype(jnp.bfloat16), 'fsdp', scatter_dimension...  108 us
    reduce_scatter x1, waiting for transfers between devices, per_device(): lax.psum_scatter(grad_fc1.astype(jnp.bfloat16), 'fsdp', scatter_dimension...  101 us
    all_to_all x1, blocking collectives, per_device(): lax.all_to_all(stacked, 'seq', split_axis=1, concat_axis=3, tiled=True)  66.9 us
    all_gather x1, waiting for transfers between devices, per_device(): lax.all_gather(w_qkv, 'fsdp', axis=0, tiled=True)  64.3 us
    all_to_all x1, waiting for transfers between devices, per_device(): lax.all_to_all(joined, 'seq', split_axis=3, concat_axis=1, tiled=True)  53.6 us
    all_gather x1, waiting for transfers between devices, per_device(): lax.all_gather(w_ada, 'fsdp', axis=0, tiled=True)  53.2 us
  transfers between devices with their start and end apart: 17, of which 10 were waited for; matrix products, arithmetic and copies ran while one was open for 29% of the time, Pallas kernels for 0%

commit v1 on v0

v1 whole, which is shorter than its diff:
```python
import math

import jax
import jax.numpy as jnp
from jax import lax
from jax.experimental import pallas as pl
from jax.experimental.pallas import tpu as pltpu
from jax.sharding import PartitionSpec as P

HD = 72
PAIR = 2 * HD
FACTOR = 1.0 / math.sqrt(HD)
FLOAT = jnp.float32
LOW = jnp.bfloat16
SWAP = [(0, 1), (1, 0)]


def contract(left, right, left_dim, right_dim):
    return lax.dot_general(
        left, right, (((left_dim,), (right_dim,)), ((), ())), preferred_element_type=FLOAT
    )


def exponentials(keys, query):
    scores = contract(keys, query, 0, 0)
    row_max = jnp.max(scores, axis=0, keepdims=True)
    exponent = jnp.exp((scores - row_max) * FACTOR)
    return exponent, 1.0 / jnp.sum(exponent, axis=0, keepdims=True)


def attend_kernel(query_ref, key_ref, value_ref, out_ref):
    query, keys, values = query_ref[0], key_ref[0], value_ref[0]
    row = lax.broadcasted_iota(jnp.int32, query.shape, 0)
    total = jnp.zeros(query.shape, FLOAT)
    for head in range(2):
        mine = (row < HD) if head == 0 else (row >= HD)
        masked = jnp.where(mine, query.astype(FLOAT), 0.0).astype(LOW)
        exponent, inverse = exponentials(keys, masked)
        mixture = contract(values, exponent.astype(LOW), 1, 0) * inverse
        total = total + jnp.where(mine, mixture, 0.0)
    out_ref[0] = total.astype(LOW)


def revisit_kernel(query_ref, key_ref, value_ref, grad_ref, dq_ref, dk_ref, dv_ref):
    query, keys, values, grad = query_ref[0], key_ref[0], value_ref[0], grad_ref[0]
    row = lax.broadcasted_iota(jnp.int32, query.shape, 0)
    d_query = jnp.zeros(query.shape, FLOAT)
    d_keys = jnp.zeros(keys.shape, FLOAT)
    d_values = jnp.zeros(keys.shape, FLOAT)
    for head in range(2):
        mine = (row < HD) if head == 0 else (row >= HD)
        masked = jnp.where(mine, query.astype(FLOAT), 0.0).astype(LOW)
        grad_masked = jnp.where(mine, grad.astype(FLOAT), 0.0).astype(LOW)
        exponent, inverse = exponentials(keys, masked)
        probs = exponent * inverse
        d_values = d_values + contract(grad_masked, probs.astype(LOW), 1, 1)
        d_probs = contract(values, grad_masked, 0, 0)
        centre = jnp.sum(probs * d_probs, axis=0, keepdims=True)
        d_scores = (probs * (d_probs - centre)).astype(LOW)
        d_query = d_query + jnp.where(mine, contract(keys, d_scores, 1, 0), 0.0)
        d_keys = d_keys + contract(masked, d_scores, 1, 1)
    dq_ref[0] = (d_query * FACTOR).astype(LOW)
    dk_ref[0] = (d_keys * FACTOR).astype(LOW)
    dv_ref[0] = d_values.astype(LOW)


def pair_spec(tokens, offset=0):
    return pl.BlockSpec((1, PAIR, tokens), lambda b, h: (b, h + offset, 0))


def attend(query, key_values):
    group, width, rows = query.shape
    length, pairs = key_values.shape[2], width // PAIR
    scores = group * width * rows * length
    return pl.pallas_call(
        attend_kernel,
        grid=(group, pairs),
        in_specs=[pair_spec(rows), pair_spec(length), pair_spec(length, pairs)],
        out_specs=pair_spec(rows),
        out_shape=jax.ShapeDtypeStruct(query.shape, LOW),
        compiler_params=pltpu.CompilerParams(vmem_limit_bytes=40 * 2**20),
        cost_estimate=pl.CostEstimate(
            flops=24 * scores, bytes_accessed=8 * query.size, transcendentals=scores // HD
        ),
    )(query, key_values, key_values)


def revisit(query, key_values, grad):
    group, width, rows = query.shape
    length, pairs = key_values.shape[2], width // PAIR
    scores = group * width * rows * length
    long_shape = jax.ShapeDtypeStruct((group, width, length), LOW)
    return pl.pallas_call(
        revisit_kernel,
        grid=(group, pairs),
        in_specs=[
            pair_spec(rows),
            pair_spec(length),
            pair_spec(length, pairs),
            pair_spec(rows),
        ],
        out_specs=(pair_spec(rows), pair_spec(length), pair_spec(length)),
        out_shape=(jax.ShapeDtypeStruct(query.shape, LOW), long_shape, long_shape),
        compiler_params=pltpu.CompilerParams(vmem_limit_bytes=40 * 2**20),
        cost_estimate=pl.CostEstimate(
            flops=48 * scores, bytes_accessed=16 * query.size, transcendentals=scores // HD
        ),
    )(query, key_values, key_values, grad)


def layer_norm(vector):
    centred = vector - jnp.mean(vector, axis=-1, keepdims=True)
    spread = jnp.mean(centred * centred, axis=-1, keepdims=True)
    return centred * lax.rsqrt(spread + 1e-06)


def modulate(vector, shift, scale):
    return layer_norm(vector) * (1.0 + scale[:, None, :]) + shift[:, None, :]


def sigmoid_linear(vector):
    return vector / (1.0 + jnp.exp(-vector))


def gelu_tanh(vector):
    return (
        0.5
        * vector
        * (1.0 + jnp.tanh(0.7978845608028654 * (vector + 0.044715 * vector * vector * vector)))
    )


def per_device(
    latents,
    condition,
    w_ada,
    b_ada,
    w_qkv,
    b_qv,
    w_proj,
    b_proj,
    w_fc1,
    b_fc1,
    w_fc2,
    b_fc2,
    grad_out,
):
    shards, halves = lax.axis_size("fsdp"), lax.axis_size("seq")
    shard, side = lax.axis_index("fsdp"), lax.axis_index("seq")
    paired = halves == 2
    model_width = w_proj.shape[1]
    own_rows = w_qkv.shape[0]
    lat_group = latents.shape[0]

    def exchange(value):
        return lax.ppermute(value, "seq", SWAP)

    def seq_sum(value):
        value = value.astype(LOW)
        if paired:
            return value.astype(FLOAT) + exchange(value).astype(FLOAT)
        return lax.psum(value.astype(FLOAT), "seq")

    def to_all(vector):
        spread = jnp.broadcast_to(vector[None], (shards,) + vector.shape)
        return lax.all_to_all(spread, "fsdp", 0, 0, tiled=True)

    def gather(weight):
        return lax.all_gather(weight, "fsdp", axis=0, tiled=True)

    def side_by_side(mine, other, axis):
        first = side == 0
        return jnp.concatenate(
            [jnp.where(first, mine, other), jnp.where(first, other, mine)], axis=axis
        )

    def scatter(value):
        return lax.psum_scatter(value.astype(LOW), "fsdp", scatter_dimension=0, tiled=True)

    if paired:
        half_rows = w_fc2.shape[0] // 2
        half_fc2 = lax.dynamic_slice_in_dim(w_fc2, side * half_rows, half_rows, 0)
        mine_fc2 = gather(half_fc2).reshape(shards, half_rows, model_width)
        full_fc2 = side_by_side(mine_fc2, exchange(mine_fc2), 1).reshape(-1, model_width)
    else:
        full_fc2 = gather(w_fc2)
    full_qkv = gather(w_qkv)
    full_proj = gather(w_proj)
    full_fc1 = gather(w_fc1)

    small = (condition.reshape(-1), b_ada, b_qv, b_proj, b_fc1, b_fc2)
    sizes = [part.shape[0] for part in small]
    packed = to_all(jnp.concatenate(small))
    edges = [sum(sizes[: i + 1]) for i in range(len(sizes) - 1)]
    parts = jnp.split(packed, edges, axis=1)
    all_conditions = parts[0].reshape(shards * lat_group, model_width).astype(FLOAT)
    bias_ada, bias_qv, bias_proj, bias_fc1, bias_fc2 = [
        part.reshape(-1).astype(FLOAT) for part in parts[1:]
    ]
    cond_own = lax.dynamic_slice_in_dim(
        sigmoid_linear(all_conditions).astype(LOW), shard * own_rows, own_rows, 1
    )
    partial_modulation = jnp.dot(cond_own, w_ada, preferred_element_type=FLOAT)
    partial_modulation = lax.all_to_all(
        partial_modulation.reshape(shards, lat_group, -1), "fsdp", 0, 0, tiled=True
    )
    modulation = jnp.sum(partial_modulation, axis=0) + bias_ada
    shift_a, scale_a, gate_a, shift_m, scale_m, gate_m = jnp.split(modulation, 6, axis=1)

    tokens = latents.astype(FLOAT)
    tok_rows = tokens.shape[1]
    normed = modulate(tokens, shift_a, scale_a).astype(LOW)
    bias_kv = jnp.concatenate([jnp.zeros((model_width,), FLOAT), bias_qv[model_width:]])
    own_kv = (
        jnp.einsum("btd,de->bet", normed, full_qkv[:, model_width:], preferred_element_type=FLOAT)
        + bias_kv[:, None]
    ).astype(LOW)
    if paired:
        key_values = jnp.concatenate([own_kv, exchange(own_kv)], axis=2)
    else:
        key_values = lax.all_gather(own_kv, "seq", axis=2, tiled=True)
    query = (
        jnp.einsum("btd,de->bet", normed, full_qkv[:, :model_width], preferred_element_type=FLOAT)
        + bias_qv[:model_width, None]
    ).astype(LOW)
    attended = attend(query, key_values)
    branch_a = jnp.einsum("bdt,de->bte", attended, full_proj, preferred_element_type=FLOAT) + bias_proj
    middle = tokens + gate_a[:, None, :] * branch_a
    normed_m = modulate(middle, shift_m, scale_m).astype(LOW)
    hidden = jnp.einsum("btd,df->btf", normed_m, full_fc1, preferred_element_type=FLOAT) + bias_fc1
    active = gelu_tanh(hidden).astype(LOW)
    cotangent = grad_out.astype(FLOAT)
    d_branch_m = (gate_m[:, None, :] * cotangent).astype(LOW)
    grad_fc2 = jnp.einsum("btf,btd->fd", active, d_branch_m, preferred_element_type=FLOAT)
    owned_fc2 = scatter(grad_fc2)
    branch_m = jnp.einsum("btf,fd->btd", active, full_fc2, preferred_element_type=FLOAT) + bias_fc2
    output = (middle + gate_m[:, None, :] * branch_m).astype(LOW)
    d_gate_m = jnp.sum(cotangent * branch_m, axis=1)
    grad_bias_fc2 = jnp.sum(d_branch_m, axis=(0, 1), dtype=FLOAT)
    d_active = jnp.einsum("btd,fd->btf", d_branch_m, full_fc2, preferred_element_type=FLOAT)
    gelu_unused, gelu_pull = jax.vjp(gelu_tanh, hidden)
    d_hidden = gelu_pull(d_active)[0].astype(LOW)
    grad_bias_fc1 = jnp.sum(d_hidden, axis=(0, 1), dtype=FLOAT)

    def grad_fc1_of(columns):
        return jnp.einsum("btd,btf->df", normed_m, columns, preferred_element_type=FLOAT)

    if paired:
        half = d_hidden.shape[2] // 2
        sent = exchange(
            grad_fc1_of(lax.dynamic_slice_in_dim(d_hidden, (1 - side) * half, half, 2)).astype(LOW)
        )
        kept = grad_fc1_of(lax.dynamic_slice_in_dim(d_hidden, side * half, half, 2))
    else:
        owned_fc1 = seq_sum(scatter(grad_fc1_of(d_hidden)))
    d_normed_m = jnp.einsum("btf,df->btd", d_hidden, full_fc1, preferred_element_type=FLOAT)
    norm_unused, pull_second = jax.vjp(modulate, middle, shift_m, scale_m)
    d_middle_norm, d_shift_m, d_scale_m = pull_second(d_normed_m)
    d_middle = cotangent + d_middle_norm
    d_gate_a = jnp.sum(d_middle * branch_a, axis=1)
    d_branch_a = (gate_a[:, None, :] * d_middle).astype(LOW)
    grad_proj = jnp.einsum("bdt,bte->de", attended, d_branch_a, preferred_element_type=FLOAT)
    owned_proj = scatter(grad_proj)
    grad_bias_proj = jnp.sum(d_branch_a, axis=(0, 1), dtype=FLOAT)
    d_attended = jnp.einsum(
        "bte,de->bdt", d_branch_a, full_proj, preferred_element_type=FLOAT
    ).astype(LOW)
    d_query, d_keys, d_values = revisit(query, key_values, d_attended)
    if paired:
        sent, d_query, d_keys, d_values = lax.optimization_barrier(
            (sent, d_query, d_keys, d_values)
        )
        half_fc1 = scatter(kept + sent.astype(FLOAT))
        owned_fc1 = side_by_side(half_fc1, exchange(half_fc1), 1).astype(FLOAT)
        away = jnp.concatenate([d_keys[:, :, tok_rows:], d_values[:, :, tok_rows:]], axis=1)
        home = jnp.concatenate([d_keys[:, :, :tok_rows], d_values[:, :, :tok_rows]], axis=1)
        d_kv = (home.astype(FLOAT) + exchange(away).astype(FLOAT)).astype(LOW)
    else:
        d_kv = lax.psum_scatter(
            jnp.concatenate([d_keys, d_values], axis=1), "seq", scatter_dimension=2, tiled=True
        )
    d_joined = jnp.concatenate([d_query, d_kv], axis=1)
    grad_qkv = jnp.einsum("btd,bet->de", normed, d_joined, preferred_element_type=FLOAT)
    owned_qkv = scatter(grad_qkv)
    column_sums = jnp.sum(d_joined, axis=(0, 2), dtype=FLOAT)
    grad_bias_qv = jnp.concatenate([column_sums[:model_width], column_sums[2 * model_width :]])
    d_normed_a = jnp.einsum("bet,de->btd", d_joined, full_qkv, preferred_element_type=FLOAT)
    first_unused, pull_first = jax.vjp(modulate, tokens, shift_a, scale_a)
    d_tokens_norm, d_shift_a, d_scale_a = pull_first(d_normed_a)
    grad_latents = d_middle + d_tokens_norm

    d_mod_part = jnp.concatenate(
        [d_shift_a, d_scale_a, d_gate_a, d_shift_m, d_scale_m, d_gate_m], axis=1
    )
    bias_parts = (grad_bias_qv, grad_bias_proj, grad_bias_fc1, grad_bias_fc2)
    chunks = jnp.concatenate([part.reshape(shards, -1) for part in bias_parts], axis=1)
    mod_size = d_mod_part.size
    flat = seq_sum(jnp.concatenate([d_mod_part.reshape(-1), chunks.reshape(-1)])).astype(LOW)
    spread = jnp.concatenate(
        [
            jnp.broadcast_to(flat[None, :mod_size], (shards, mod_size)),
            flat[mod_size:].reshape(shards, -1),
        ],
        axis=1,
    )
    arrived = lax.all_to_all(spread, "fsdp", 0, 0, tiled=True)
    d_modulation = arrived[:, :mod_size].reshape(shards * lat_group, -1)
    owned_chunks = jnp.sum(arrived[:, mod_size:], axis=0, dtype=FLOAT)
    bias_edges = [
        b_qv.shape[0],
        b_qv.shape[0] + b_proj.shape[0],
        b_qv.shape[0] + b_proj.shape[0] + b_fc1.shape[0],
    ]
    owned_qv, owned_bproj, owned_bfc1, owned_bfc2 = jnp.split(owned_chunks, bias_edges)
    owned_ada = jnp.einsum("lk,le->ke", cond_own, d_modulation, preferred_element_type=FLOAT)
    owned_bada = lax.dynamic_slice_in_dim(
        jnp.sum(d_modulation, axis=0, dtype=FLOAT), shard * b_ada.shape[0], b_ada.shape[0], 0
    )
    d_cond = jnp.einsum("le,ke->lk", d_modulation, w_ada, preferred_element_type=FLOAT)
    d_cond = lax.all_to_all(
        d_cond.reshape(shards, lat_group, own_rows), "fsdp", 0, 0, tiled=True
    )
    d_cond = jnp.moveaxis(d_cond, 0, 1).reshape(lat_group, model_width)
    silu_unused, silu_pull = jax.vjp(sigmoid_linear, condition.astype(FLOAT))
    grad_condition = silu_pull(d_cond)[0]
    return (
        output,
        grad_latents,
        grad_condition,
        owned_ada,
        owned_bada,
        seq_sum(owned_qkv),
        owned_qv,
        seq_sum(owned_proj),
        owned_bproj,
        owned_fc1,
        owned_bfc1,
        seq_sum(owned_fc2),
        owned_bfc2,
    )


def solution(mesh):
    return jax.shard_map(
        per_device,
        mesh=mesh,
        in_specs=(
            P("fsdp", "seq", None),
            P("fsdp", None),
            P("fsdp", None),
            P("fsdp"),
            P("fsdp", None),
            P("fsdp"),
            P("fsdp", None),
            P("fsdp"),
            P("fsdp", None),
            P("fsdp"),
            P("fsdp", None),
            P("fsdp"),
            P("fsdp", "seq", None),
        ),
        out_specs=(
            P("fsdp", "seq", None),
            P("fsdp", "seq", None),
            P("fsdp", None),
            P("fsdp", None),
            P("fsdp"),
            P("fsdp", None),
            P("fsdp"),
            P("fsdp", None),
            P("fsdp"),
            P("fsdp", None),
            P("fsdp"),
            P("fsdp", None),
            P("fsdp"),
        ),
        check_vma=False,
    )
```

time: 1320 us -> 787 us (0.60)
  blocking collectives: 242 us -> 0 us
  waiting for transfers between devices: 594 us -> 463 us
  matrix products: 233 us -> 133 us
  local copies, waits for them, and re-layouts: 125 us -> 26.9 us
  Pallas kernels: 0 us -> 53.2 us
  other arithmetic: 81.7 us -> 58.4 us
  starting transfers between devices: 14.7 us -> 28.3 us
    reduce_scatter x4 -> x2, waiting for transfers between devices: 319 us -> 44 us  [scatter(): lax.psum_scatter(value.astype(LOW), 'fsdp', scatter_dimension=0, tiled=True)]
    ppermute x0 -> x9, waiting for transfers between devices: none -> 169 us  [exchange(): return lax.ppermute(value, 'seq', SWAP)]
    unnamed x2 -> x0, blocking collectives: 127 us -> none
    dot_general x28 -> x17, matrix products: 233 us -> 133 us  [the longest x1 18.3 us: per_device(): jnp.einsum('btf,fd->btd', active, full_fc2, preferred_element_type=FLOAT)]
    all_to_all x1 -> x0, blocking collectives: 66.9 us -> none  [per_device(): lax.all_to_all(stacked, 'seq', split_axis=1, concat_axis=3, tiled=True)]
    pallas_call x0 -> x2, Pallas kernels: none -> 53.2 us  [the longest x1 37.3 us: revisit(): pl.pallas_call(revisit_kernel, grid=(group, pairs), in_specs=[pair_spec(r...]
    unnamed x19 -> x10, waiting for transfers between devices: 52.6 us -> 104 us
    all_to_all x3 -> x4, waiting for transfers between devices: 80.3 us -> 33.5 us  [the longest x1 12.4 us: per_device(): arrived = lax.all_to_all(spread, 'fsdp', 0, 0, tiled=True)]
  transfers between devices with their start and end apart: 17 -> 21, of which waited for: 10 -> 15; matrix products, arithmetic and copies ran while one was open for 29% -> 22% of each run, Pallas kernels for 0% -> 7%
where the time goes in v1:
time: 787 us; the launch traced here: 778 us
  waiting for transfers between devices  463 us (59%)
  matrix products  133 us (17%)
  other arithmetic  58.4 us (7%)
  Pallas kernels  53.2 us (7%)
  starting transfers between devices  28.3 us (4%)
  local copies, waits for them, and re-layouts  26.9 us (3%)
  between operations  15.3 us (2%)
    ppermute x9, waiting for transfers between devices, exchange(): return lax.ppermute(value, 'seq', SWAP)  169 us
    all_gather x4, waiting for transfers between devices, gather(): return lax.all_gather(weight, 'fsdp', axis=0, tiled=True)  113 us
    unnamed x10, waiting for transfers between devices  104 us
    reduce_scatter x2, waiting for transfers between devices, scatter(): lax.psum_scatter(value.astype(LOW), 'fsdp', scatter_dimension=0, tiled=True)  44 us
    pallas_call x1, Pallas kernels, revisit(): pl.pallas_call(revisit_kernel, grid=(group, pairs), in_specs=[pair_spec(r...  37.3 us
    dot_general x1, matrix products, per_device(): jnp.einsum('btf,fd->btd', active, full_fc2, preferred_element_type=FLOAT)  18.3 us
    dot_general x1, matrix products, per_device(): jnp.einsum('btd,fd->btf', d_branch_m, full_fc2, preferred_element_type=FL...  17.6 us
    pallas_call x1, Pallas kernels, attend(): pl.pallas_call(attend_kernel, grid=(group, pairs), in_specs=[pair_spec(ro...  15.9 us
  transfers between devices with their start and end apart: 21, of which 15 were waited for; matrix products, arithmetic and copies ran while one was open for 22% of the time, Pallas kernels for 7%

profile of v1, /device:TPU:0, one launch (start us, length us, event | category | flops | bytes accessed | tf_op | source)
XLA Modules:
  0.0 778.2 jit_solution(14357921082606737360)
XLA Ops:
  11.2 58.7 %all-gather.11.cloned.1.call-done = bf16[2304,1152]{1,0:T(8,128)(2,1)} async-done(((bf16[144,1152]{1,0:T(8,128)(2,1)}), bf16[2304,1152]{1,0:T(8,128)(2,1)}) %all-gather.11.cloned.1.call-update) | async-done | bytes 5308432 | tf_op jit(solution)/shard_map/all_gather | solution.py:169
  96.6 12.2 %all-to-all-done.1 = f32[16,1,6912]{2,1,0:T(1,128)S(1)} async-done(((f32[16,1,6912]{2,1,0:T(1,128)}), f32[16,1,6912]{2,1,0:T(1,128)S(1)}, u32[]{:S(2)}, u32[]{:S(2)}) %all-to-all-start.1) | async-done | bytes 442400 | tf_op jit(solution)/shard_map/all_to_all | solution.py:204
  109.3 38.6 %all-gather.5.cloned.1.call-done = bf16[1152,3456]{1,0:T(8,128)(2,1)} async-done(((bf16[72,3456]{1,0:T(8,128)(2,1)}), bf16[1152,3456]{1,0:T(8,128)(2,1)}) %all-gather.5.cloned.1.call-update) | async-done | bytes 7962640 | tf_op jit(solution)/shard_map/all_gather | solution.py:169
  160.5 26.9 %collective-permute-done.1 = bf16[16,144,1152]{2,1,0:T(8,128)(2,1)} collective-permute-done((bf16[16,144,1152]{2,1,0:T(8,128)(2,1)}, bf16[16,144,1152]{2,1,0:T(8,128)(2,1)}, u32[]{:S(2)}, u32[]{:S(2)}) %collective-permute-start.1) | collective-permute-done | bytes 5308448 | tf_op jit(solution)/shard_map/ppermute | solution.py:156
  187.5 9.2 %broadcast_select_fusion.1 = (bf16[16,144,1152]{2,1,0:T(8,128)(2,1)}, bf16[16,144,1152]{2,1,0:T(8,128)(2,1)}) fusion(bf16[16,144,1152]{2,1,0:T(8,128)(2,1)} %bitcast.113, bf16[16,144,1152]{2,1,0:T(8,128)(2,1)} %collective-permute-done.1, pred[]{:T(512)S(6)} %eq.4), kind=kLoop, calls=%fused_computation.21 | loop fusion | flops 5308416 | bytes 21233664 | tf_op jit(solution)/shard_map/jit(_where)/select_n | solution.py:174
  196.6 9.8 %pad_maximum_fusion = bf16[16,288,1152]{2,1,0:T(8,128)(2,1)} fusion(bf16[16,144,1152]{2,1,0:T(8,128)(2,1)} %get-tuple-element.46, bf16[16,144,1152]{2,1,0:T(8,128)(2,1)} %get-tuple-element.45), kind=kLoop, calls=%fused_computation.7 | loop fusion | flops 21233664 | bytes 21233664 | tf_op jit(solution)/shard_map/concatenate | solution.py:173
  206.4 30.9 %collective-permute-done = bf16[1,2304,512]{2,1,0:T(8,128)(2,1)} collective-permute-done((bf16[1,2304,512]{2,1,0:T(8,128)(2,1)}, bf16[1,2304,512]{2,1,0:T(8,128)(2,1)}, u32[]{:S(2)}, u32[]{:S(2)}) %collective-permute-start) | collective-permute-done | bytes 2359328 | tf_op jit(solution)/shard_map/ppermute | solution.py:156
  240.4 15.9 %shard_map.228 = bf16[1,1152,512]{2,1,0:T(8,128)(2,1)S(1)} custom-call(bf16[1,1152,512]{2,1,0:T(8,128)(2,1)S(1)} %fusion.26.query_ref, bf16[1,2304,1024]{2,1,0:T(8,128)(2,1)S(1)} %pad_maximum_fusion.1.key_ref.value_ref, bf16[1,2304,1024]{2,1,0:T(8,128)(2,1)S(1)} %pad_maximum_fusion.1.key_ref.value_ref), custom_call_target="tpu_custom_call" | custom-call | flops 14495514624 | bytes 4718592 | tf_op jit(solution)/shard_map/pallas_call | solution.py:75
  265.7 15.6 %all-gather.9.cloned.1.call-done = bf16[1152,4608]{1,0:T(8,128)(2,1)} async-done(((bf16[72,4608]{1,0:T(8,128)(2,1)}), bf16[1152,4608]{1,0:T(8,128)(2,1)}) %all-gather.9.cloned.1.call-update) | async-done | bytes 10616848 | tf_op jit(solution)/shard_map/all_gather | solution.py:169
  281.4 12.3 %fusion.92 = f32[512,4608]{1,0:T(8,128)} fusion(bf16[1152,4608]{1,0:T(8,128)(2,1)} %all-gather.9.cloned.1.call-done, f32[1,512,1152]{2,1,0:T(8,128)} %copy-done.8, f32[1152]{0:T(1024)S(1)} %get-tuple-element.34, f32[1152]{0:T(1024)S(1)} %get-tuple-element.35, f32[512]{0:T(512)S(1)} %fusion.70, f32[512]{0:T(512)S(1)} %broadcast_multiply_fusion), kind=kOutput, calls=%fused_computation.158 | convolution fusion | flops 5438767104 | bytes 22426624 | tf_op jit(solution)/shard_map/btd,df->btf/dot_general | solution.py:230
  293.7 17.6 %fusion.89 = (bf16[4608]{0:T(1024)(128)(2,1)S(1)}, bf16[512,4608]{1,0:T(8,128)(2,1)S(1)}) fusion(bf16[4608,1152]{1,0:T(8,128)(2,1)} %bitcast.110, bf16[1,512,1152]{2,1,0:T(8,128)(2,1)S(1)} %copy-done.19, f32[1152]{0:T(1024)S(1)} %get-tuple-element.33, f32[512,4608]{1,0:T(8,128)} %fusion.92, f32[4608]{0:T(1024)S(1)} %reshape.491), kind=kOutput, calls=%fused_computation.157 | convolution fusion | flops 5498924544 | bytes 25984512 | tf_op jit(solution)/shard_map/btd,fd->btf/dot_general | solution.py:240
  318.3 11.8 %fusion.37 = (bf16[1152]{0:T(1024)(128)(2,1)S(1)}, f32[512]{0:T(512)S(1)}, f32[512,1152]{1,0:T(8,128)S(1)}) fusion(f32[1,512,1152]{2,1,0:T(8,128)S(1)} %copy-done.9, f32[512]{0:T(512)S(1)} %fusion.70, f32[512]{0:T(512)S(1)} %broadcast_multiply_fusion, f32[1152]{0:T(1024)S(1)} %get-tuple-element.35, bf16[512,4608]{1,0:T(8,128)(2,1)} %copy-done.35, ...), kind=kOutput, calls=%fused_computation.62 | convolution fusion | flops 5439945216 | bytes 20067072 | tf_op jit(solution)/shard_map/btf,df->btd/dot_general | solution.py:256
  342.4 37.3 %shard_map.229 = (bf16[1,1152,512]{2,1,0:T(8,128)(2,1)S(1)}, bf16[1,1152,1024]{2,1,0:T(8,128)(2,1)S(1)}, bf16[1,1152,1024]{2,1,0:T(8,128)(2,1)S(1)}) custom-call(bf16[1,1152,512]{2,1,0:T(8,128)(2,1)S(1)} %copy-done.7, bf16[1,2304,1024]{2,1,0:T(8,128)(2,1)S(1)} %copy-done.2, bf16[1,2304,1024]{2,1,0:T(8,128)(2,1)S(1)} %copy-done.2, ...), custom_call_target="tpu_custom_call" | custom-call | flops 28991029248 | bytes 9437184 | tf_op jit(solution)/shard_map/pallas_call | solution.py:93
  386.1 47.7 %collective-permute-done.2 = bf16[1152,2304]{1,0:T(8,128)(2,1)} collective-permute-done((bf16[1152,2304]{1,0:T(8,128)(2,1)}, bf16[1152,2304]{1,0:T(8,128)(2,1)}, u32[]{:S(2)}, u32[]{:S(2)}) %collective-permute-start.2) | collective-permute-done | bytes 5308448 | tf_op jit(solution)/shard_map/ppermute | solution.py:156
  433.8 9.0 %add_convert_fusion = bf16[1152,2304]{1,0:T(8,128)(2,1)} fusion(f32[1152,2304]{1,0:T(8,128)} %fusion.41, bf16[1152,2304]{1,0:T(8,128)(2,1)} %collective-permute-done.2), kind=kLoop, calls=%fused_computation.8 | loop fusion | flops 7962624 | bytes 21233664 | tf_op jit(solution)/shard_map/convert_element_type | solution.py:178
  442.8 13.7 %convolution_convert_fusion = bf16[4608,1152]{1,0:T(8,128)(2,1)} fusion(bf16[1,512,1152]{2,1,0:T(8,128)(2,1)} %param.25, f32[1152]{0:T(1024)S(1)} %get-tuple-element.33, f32[512,4608]{1,0:T(8,128)} %fusion.92, f32[4608]{0:T(1024)S(1)} %reshape.491), kind=kOutput, calls=%fused_computation | convolution fusion | flops 5466488832 | bytes 21256704 | tf_op jit(solution)/shard_map/btf,btd->fd/dot_general | solution.py:234
  463.9 50.9 %collective-permute-done.3 = bf16[1,2304,512]{2,1,0:T(8,128)(2,1)} collective-permute-done((bf16[1,2304,512]{2,1,0:T(8,128)(2,1)}, bf16[1,2304,512]{2,1,0:T(8,128)(2,1)}, u32[]{:S(2)}, u32[]{:S(2)}) %collective-permute-start.3) | collective-permute-done | bytes 2359328 | tf_op jit(solution)/shard_map/ppermute | solution.py:156
  519.4 8.5 %convolution_convert_fusion.1 = bf16[1152,3456]{1,0:T(8,128)(2,1)} fusion(bf16[1,2304,512]{2,1,0:T(8,128)(2,1)S(1)} %add_convert_fusion.1, bf16[1,1152,512]{2,1,0:T(8,128)(2,1)S(1)} %copy-done.5, bf16[1,512,1152]{2,1,0:T(8,128)(2,1)S(1)} %copy-done.13, f32[1152]{0:T(1024)S(1)} %copy-done.34, f32[1152]{0:T(1024)S(1)} %copy-done.24, f32[512]{0:T(512)S(1)} %copy-done.32, ...), kind=kOutput, calls=%fused_computation.1 | convolution fusion | flops 4091461632 | bytes 12694528 | tf_op jit(solution)/shard_map/btd,bet->de/dot_general | solution.py:283
  528.0 11.4 %fusion.34 = (f32[512]{0:T(512)S(1)}, f32[512,1152]{1,0:T(8,128)}) fusion(bf16[1,512,1152]{2,1,0:T(8,128)(2,1)S(1)} %copy-done.13, f32[1152]{0:T(1024)S(1)} %copy-done.24, f32[512]{0:T(512)S(1)} %copy-done.27, bf16[1152,3456]{1,0:T(8,128)(2,1)} %all-gather.5.cloned.1.call-done, bf16[1,2304,512]{2,1,0:T(8,128)(2,1)} %copy-done.18, ...), kind=kOutput, calls=%fused_computation.57 | convolution fusion | flops 4086889984 | bytes 15049216 | tf_op jit(solution)/shard_map/bet,de->btd/dot_general | solution.py:287
  548.5 18.3 %fusion.36 = (bf16[1152]{0:T(1024)(128)(2,1)S(1)}, bf16[1152]{0:T(1024)(128)(2,1)S(1)}, f32[1,512,1152]{2,1,0:T(8,128)}, bf16[1,512,1152]{2,1,0:T(8,128)(2,1)}) fusion(bf16[1,512,1152]{2,1,0:T(8,128)(2,1)} %param.25, f32[512,1152]{1,0:T(8,128)} %get-tuple-element.64, f32[1,512,1152]{2,1,0:T(8,128)} %copy-done.15, f32[512]{0:T(512)S(1)} %negate_multiply_fusion.1, ...), kind=kOutput, calls=%fused_computation.59 | convolution fusion | flops 5471205376 | bytes 35436544 | tf_op jit(solution)/shard_map/btf,fd->btd/dot_general | solution.py:236
  578.4 12.4 %all-to-all-done.2 = bf16[16,2,3744]{2,1,0:T(2,128)(2,1)S(1)} async-done(((bf16[16,2,3744]{2,1,0:T(2,128)(2,1)}), bf16[16,2,3744]{2,1,0:T(2,128)(2,1)S(1)}, u32[]{:S(2)}, u32[]{:S(2)}) %all-to-all-start.2) | async-done | bytes 239648 | tf_op jit(solution)/shard_map/all_to_all | solution.py:306
  607.5 44.0 %reduce-scatter.11.cloned.1.call-done = bf16[288,1152]{1,0:T(8,128)(2,1)} async-done(((bf16[4608,1152]{1,0:T(8,128)(2,1)}), bf16[288,1152]{1,0:T(8,128)(2,1)}) %reduce-scatter.11.cloned.1.call-update) | async-done | bytes 663568 | tf_op jit(solution)/shard_map/reduce_scatter | solution.py:178
  655.1 101.6 %reduce-scatter.13.cloned.1.call-done = bf16[72,3456]{1,0:T(8,128)(2,1)} async-done(((bf16[1152,3456]{1,0:T(8,128)(2,1)}), bf16[72,3456]{1,0:T(8,128)(2,1)}) %reduce-scatter.13.cloned.1.call-update) | async-done | bytes 497680
  759.4 10.5 %collective-permute-done.5 = bf16[72,3456]{1,0:T(8,128)(2,1)S(1)} collective-permute-done((bf16[72,3456]{1,0:T(8,128)(2,1)}, bf16[72,3456]{1,0:T(8,128)(2,1)S(1)}, u32[]{:S(2)}, u32[]{:S(2)}) %collective-permute-start.5) | collective-permute-done | bytes 497696 | tf_op jit(solution)/shard_map/ppermute | solution.py:156
  (213 shorter events, 138.1 us)
Async XLA Ops:
  7.2 82.9 %copy-start = (bf16[72,6912]{1,0:T(8,128)(2,1)S(1)}, bf16[72,6912]{1,0:T(8,128)(2,1)}, u32[]{:S(2)}) copy-start(bf16[72,6912]{1,0:T(8,128)(2,1)} %param.15) | copy-start | bytes 2985988
  7.2 62.7 %all-gather.11.cloned.1.call-start = ((), (), s32[]{:S(2)}) async-start(), calls=%async_computation.11 | async-start | bytes 5640192 | tf_op jit(solution)/shard_map/all_gather | solution.py:169
  9.2 138.8 %all-gather.5.cloned.1.call-start = ((), (), s32[]{:S(2)}) async-start(), calls=%async_computation.8 | async-start | bytes 8460288 | tf_op jit(solution)/shard_map/all_gather | solution.py:169
  9.9 248.4 %all-gather.7.cloned.1.call-start = ((), (), s32[]{:S(2)}) async-start(), calls=%async_computation.9 | async-start | bytes 2820096 | tf_op jit(solution)/shard_map/all_gather | solution.py:169
  10.6 270.7 %all-gather.9.cloned.1.call-start = ((), (), s32[]{:S(2)}) async-start(), calls=%async_computation.10 | async-start | bytes 11280384 | tf_op jit(solution)/shard_map/all_gather | solution.py:169
  69.9 117.6 %collective-permute-start.1 = (bf16[16,144,1152]{2,1,0:T(8,128)(2,1)}, bf16[16,144,1152]{2,1,0:T(8,128)(2,1)}, u32[]{:S(2)}, u32[]{:S(2)}) collective-permute-start(bf16[16,144,1152]{2,1,0:T(8,128)(2,1)} %bitcast.112), channel_id=1, source_target_pairs={{0,1},{1,0},{2,3},{3,2},{4,5},{5,4},{6,7},{7,6},{8,9},{9,8},{10,11... | collective-permute-start | bytes 15925256 | tf_op jit(solution)/shard_map/ppermute | solution.py:156
  78.0 12.0 %all-to-all-start = ((bf16[16,2,1080]{2,1,0:T(2,128)(2,1)}), bf16[16,2,1080]{2,1,0:T(2,128)(2,1)S(1)}, u32[]{:S(2)}, u32[]{:S(2)}) async-start(bf16[16,2,1080]{2,1,0:T(2,128)(2,1)} %reshape.513), calls=%async_computation | async-start | bytes 147456 | tf_op jit(solution)/shard_map/all_to_all | solution.py:166
  91.7 17.2 %all-to-all-start.1 = ((f32[16,1,6912]{2,1,0:T(1,128)}), f32[16,1,6912]{2,1,0:T(1,128)S(1)}, u32[]{:S(2)}, u32[]{:S(2)}) async-start(f32[16,1,6912]{2,1,0:T(1,128)} %copy.34), calls=%async_computation.1 | async-start | bytes 884736 | tf_op jit(solution)/shard_map/all_to_all | solution.py:204
  95.3 473.3 %reduce-scatter.15.cloned.1.call-start = ((), (), s32[]{:S(2)}) async-start(), calls=%async_computation.15 | async-start | bytes 2820096
  155.4 82.0 %collective-permute-start = (bf16[1,2304,512]{2,1,0:T(8,128)(2,1)}, bf16[1,2304,512]{2,1,0:T(8,128)(2,1)}, u32[]{:S(2)}, u32[]{:S(2)}) collective-permute-start(bf16[1,2304,512]{2,1,0:T(8,128)(2,1)} %fusion.14), channel_id=1, source_target_pairs={{0,1},{1,0},{2,3},{3,2},{4,5},{5,4},{6,7},{7,6},{8,9},{9,8},{10,11... | collective-permute-start | bytes 7077896 | tf_op jit(solution)/shard_map/ppermute | solution.py:156
  160.5 79.8 %copy-start.6 = (bf16[1,1152,512]{2,1,0:T(8,128)(2,1)}, bf16[1,1152,512]{2,1,0:T(8,128)(2,1)S(1)}, u32[]{:S(2)}) copy-start(bf16[1,1152,512]{2,1,0:T(8,128)(2,1)S(1)} %fusion.26.query_ref) | copy-start | bytes 3538948
  316.9 116.9 %collective-permute-start.2 = (bf16[1152,2304]{1,0:T(8,128)(2,1)}, bf16[1152,2304]{1,0:T(8,128)(2,1)}, u32[]{:S(2)}, u32[]{:S(2)}) collective-permute-start(bf16[1152,2304]{1,0:T(8,128)(2,1)} %convolution_convert_fusion.2), channel_id=1, source_target_pairs={{0,1},{1,0},{2,3},{3,2},{4,5},{5,4},{6,7},{7,6},{8,9},{9,8},{10,11... | collective-permute-start | bytes 15925256 | tf_op jit(solution)/shard_map/ppermute | solution.py:156
  336.2 269.2 %reduce-scatter.9.cloned.1.call-start = ((), (), s32[]{:S(2)}) async-start(), calls=%async_computation.12 | async-start | bytes 5640192 | tf_op jit(solution)/shard_map/reduce_scatter | solution.py:178
  442.8 208.6 %reduce-scatter.11.cloned.1.call-start = ((), (), s32[]{:S(2)}) async-start(), calls=%async_computation.13 | async-start | bytes 11280384 | tf_op jit(solution)/shard_map/reduce_scatter | solution.py:178
  456.6 300.1 %reduce-scatter.13.cloned.1.call-start = ((), (), s32[]{:S(2)}) async-start(), calls=%async_computation.14 | async-start | bytes 8460288
  461.9 52.9 %collective-permute-start.3 = (bf16[1,2304,512]{2,1,0:T(8,128)(2,1)}, bf16[1,2304,512]{2,1,0:T(8,128)(2,1)}, u32[]{:S(2)}, u32[]{:S(2)}) collective-permute-start(bf16[1,2304,512]{2,1,0:T(8,128)(2,1)} %pad_maximum_fusion.3), channel_id=1, source_target_pairs={{0,1},{1,0},{2,3},{3,2},{4,5},{5,4},{6,7},{7,6},{8,9},{9,8},{10,11... | collective-permute-start | bytes 7077896 | tf_op jit(solution)/shard_map/ppermute | solution.py:156
  567.0 4.3 collective-permute-start.4
  568.6 8.2 %collective-permute-start.6 = (bf16[72,1152]{1,0:T(8,128)(2,1)}, bf16[72,1152]{1,0:T(8,128)(2,1)S(1)}, u32[]{:S(2)}, u32[]{:S(2)}) collective-permute-start(bf16[72,1152]{1,0:T(8,128)(2,1)} %reduce-scatter.15.cloned.1.call-done), channel_id=1, source_target_pairs={{0,1},{1,0},{2,3},{3,2},{4,5},{5,4},{6,7},{7,6},{8,9},{9,8},{10,11... | collective-permute-start | bytes 497672 | tf_op jit(solution)/shard_map/ppermute | solution.py:156
  573.2 17.7 %all-to-all-start.2 = ((bf16[16,2,3744]{2,1,0:T(2,128)(2,1)}), bf16[16,2,3744]{2,1,0:T(2,128)(2,1)S(1)}, u32[]{:S(2)}, u32[]{:S(2)}) async-start(bf16[16,2,3744]{2,1,0:T(2,128)(2,1)} %reshape.515), calls=%async_computation.2 | async-start | bytes 491520 | tf_op jit(solution)/shard_map/all_to_all | solution.py:306
  592.3 11.8 %all-to-all-start.3 = ((f32[16,1,72]{2,1,0:T(1,128)}), f32[16,1,72]{2,1,0:T(1,128)S(1)}, u32[]{:S(2)}, u32[]{:S(2)}) async-start(f32[16,1,72]{2,1,0:T(1,128)} %bitcast.29), calls=%async_computation.3 | async-start | bytes 16384 | tf_op jit(solution)/shard_map/all_to_all | solution.py:320
  605.4 47.5 %collective-permute-start.7 = (bf16[72,2304]{1,0:T(8,128)(2,1)}, bf16[72,2304]{1,0:T(8,128)(2,1)S(1)}, u32[]{:S(2)}, u32[]{:S(2)}) collective-permute-start(bf16[72,2304]{1,0:T(8,128)(2,1)} %reduce-scatter.9.cloned.1.call-done), channel_id=1, source_target_pairs={{0,1},{1,0},{2,3},{3,2},{4,5},{5,4},{6,7},{7,6},{8,9},{9,8},{10,11... | collective-permute-start | bytes 995336 | tf_op jit(solution)/shard_map/ppermute | solution.py:156
  651.4 106.7 %copy-start.20 = (bf16[288,1152]{1,0:T(8,128)(2,1)S(1)}, bf16[288,1152]{1,0:T(8,128)(2,1)}, u32[]{:S(2)}) copy-start(bf16[288,1152]{1,0:T(8,128)(2,1)} %reduce-scatter.11.cloned.1.call-done) | copy-start | bytes 1990660
  651.4 106.7 %collective-permute-start.8 = (bf16[288,1152]{1,0:T(8,128)(2,1)}, bf16[288,1152]{1,0:T(8,128)(2,1)S(1)}, u32[]{:S(2)}, u32[]{:S(2)}) collective-permute-start(bf16[288,1152]{1,0:T(8,128)(2,1)} %reduce-scatter.11.cloned.1.call-done), channel_id=1, source_target_pairs={{0,1},{1,0},{2,3},{3,2},{4,5},{5,4},{6,7},{7,6},{8,9},{9,8},{10,11... | collective-permute-start | bytes 1990664 | tf_op jit(solution)/shard_map/ppermute | solution.py:156
  756.7 13.2 %collective-permute-start.5 = (bf16[72,3456]{1,0:T(8,128)(2,1)}, bf16[72,3456]{1,0:T(8,128)(2,1)S(1)}, u32[]{:S(2)}, u32[]{:S(2)}) collective-permute-start(bf16[72,3456]{1,0:T(8,128)(2,1)} %reduce-scatter.13.cloned.1.call-done), channel_id=1, source_target_pairs={{0,1},{1,0},{2,3},{3,2},{4,5},{5,4},{6,7},{7,6},{8,9},{9,8},{10,11... | collective-permute-start | bytes 1493000 | tf_op jit(solution)/shard_map/ppermute | solution.py:156
  (35 other events, 575.4 us)
Sparse Core Ops, SparseCore 0:
  10.8 59.0 all-gather.10
  72.0 75.8 all-gather.4
  150.1 41.7 all-gather.6
  194.0 87.3 all-gather.8
  336.3 61.1 reduce-scatter.14
  442.9 77.6 reduce-scatter.8
  525.2 126.1 reduce-scatter.10
  656.1 100.5 reduce-scatter.12
